TPU v7x, 32 devices: a whole 2x2x4 slice. The times are simulated.
32 devices in a mesh: tile: 8 (over z, x), zslab: 4 (over y, core).
Axes of the slice: x: 2, y: 2, z: 4, core: 2. Of those that a mesh axis runs over, the one named last changes fastest.
Arguments:
- band: bfloat16 [8, 4, 128, 64, 512], P('tile', None, 'zslab'), may hold values from -6 to 6
- pairs: int32 [16, 4], replicated, may hold values from 0 to 7, as said below
- extents: int32 [16, 2], replicated, may hold values from 32 to 512, as said below
Outputs:
- maps: float32 [16, 128, 32, 256], P('tile', 'zslab')
Inputs may be any that keep to these rules, and one draw needn't show every extreme that they name: `pairs`: every slot (tile, face) with tile < 8 and face < 4 is named by exactly one pair, and a pair names two different slots. `extents`: column 0 lies in 32 to 64, column 1 in 256 to 512; some pair has both at their most.
All inputs are finite; a program needn't handle non-finite values.
Results may differ from a plain program's by a relative error of at most 0.012.
The roundings to bfloat16 on the way count: a program that leaves them out, or rounds other values in their place, can miss the bound.
Values may be sent and summed in bfloat16 or wider, within the bound.
No kernel may reach another device: no remote copies, remote signals or barrier semaphores. Data moves between devices by JAX's collectives and lax.ppermute only.
A program may use at most 64 MiB of HBM per device.

v0:
```python
import functools
import math


import jax
import jax.numpy as jnp
import numpy as np
from jax import lax
from jax.experimental import pallas as pl
from jax.experimental.pallas import tpu as pltpu
from jax.sharding import PartitionSpec as P

GX = 32
GY = 256
GZ = 128
FACES = 4


def dft_tables(length):
    indices = jnp.arange(length, dtype=jnp.int32)
    modular = indices[:, None] * indices[None, :] % length
    angles = modular.astype(jnp.float32) * (2.0 * math.pi / length)
    factor = 1.0 / math.sqrt(length)
    return (
        (jnp.cos(angles) * factor).astype(jnp.bfloat16),
        (jnp.sin(angles) * factor).astype(jnp.bfloat16),
    )


def product(form, left, right):
    return jnp.einsum(form, left, right, preferred_element_type=jnp.float32)


def reduce_resolution(image_volume, crop_bounds):
    row_mask = (
        jnp.arange(image_volume.shape[2], dtype=jnp.int32)[None, :] < crop_bounds[:, 0:1]
    ).astype(jnp.bfloat16)
    col_mask = (
        jnp.arange(image_volume.shape[3], dtype=jnp.int32)[None, :] < crop_bounds[:, 1:2]
    ).astype(jnp.bfloat16)
    masked = image_volume * row_mask[:, None, :, None] * col_mask[:, None, None, :]
    raw_cols = jnp.arange(image_volume.shape[3], dtype=jnp.int32)
    pooled_cols = jnp.arange(GY, dtype=jnp.int32)
    pooling = jnp.where(raw_cols[:, None] // 2 == pooled_cols[None, :], 0.5, 0.0).astype(
        jnp.bfloat16
    )
    along_pooled = product("szxy,yk->szxk", masked, pooling)
    shaped = along_pooled.reshape(image_volume.shape[0], image_volume.shape[1], GX, 2, GY)
    return (shaped[:, :, :, 0, :] + shaped[:, :, :, 1, :]).astype(jnp.bfloat16)


def cross_phase(owner_re, owner_im, pairs, tiles_here):
    first_dev = pairs[:, 0] // tiles_here
    first_pos = pairs[:, 0] % tiles_here * FACES + pairs[:, 1]
    second_tile_device = pairs[:, 2] // tiles_here
    second_pos = pairs[:, 2] % tiles_here * FACES + pairs[:, 3]
    first_re = owner_re[first_dev, :, first_pos].astype(jnp.float32)
    first_im = owner_im[first_dev, :, first_pos].astype(jnp.float32)
    second_re = owner_re[second_tile_device, :, second_pos].astype(jnp.float32)
    second_im = owner_im[second_tile_device, :, second_pos].astype(jnp.float32)
    cross_re = first_re * second_re + first_im * second_im
    cross_im = first_im * second_re - first_re * second_im
    scaled = jnp.sqrt(cross_re * cross_re + cross_im * cross_im + 1.0)
    return ((cross_re / scaled).astype(jnp.bfloat16), (cross_im / scaled).astype(jnp.bfloat16))


def inverse_z(phase_real_part, phase_im, tables_z):
    w_re = (
        product("pmjk,mz->pzjk", phase_real_part, tables_z[0])
        - product("pmjk,mz->pzjk", phase_im, tables_z[1])
    ).astype(jnp.bfloat16)
    w_im = (
        product("pmjk,mz->pzjk", phase_im, tables_z[0])
        + product("pmjk,mz->pzjk", phase_real_part, tables_z[1])
    ).astype(jnp.bfloat16)
    return (w_re, w_im)


def inverse_x(w_re, w_im, tables_x):
    v_re = (
        product("pzjk,jx->pzxk", w_re, tables_x[0]) - product("pzjk,jx->pzxk", w_im, tables_x[1])
    ).astype(jnp.bfloat16)
    v_im = (
        product("pzjk,jx->pzxk", w_im, tables_x[0]) + product("pzjk,jx->pzxk", w_re, tables_x[1])
    ).astype(jnp.bfloat16)
    return (v_re, v_im)


def general_shards(band, pairs, extents):
    tables_x = dft_tables(GX)
    tables_y = dft_tables(GY)
    tables_z = dft_tables(GZ)
    tiles_here = band.shape[0]
    slots = tiles_here * FACES
    zrows = band.shape[2]
    tile_pos = lax.axis_index("tile")
    global_slot = tile_pos * slots + jnp.arange(slots, dtype=jnp.int32)
    first_slot = pairs[:, 0] * FACES + pairs[:, 1]
    second_slot = pairs[:, 2] * FACES + pairs[:, 3]
    matches = (
        (first_slot[None, :] == global_slot[:, None])
        | (second_slot[None, :] == global_slot[:, None])
    ).astype(jnp.int32)
    crop_bounds = jnp.sum(matches[:, :, None] * extents[None, :, :], axis=1)
    image_volume = band.reshape(slots, zrows, 2 * GX, 2 * GY)
    reduced_volume = reduce_resolution(image_volume, crop_bounds)
    y_re = product("szxy,yk->szxk", reduced_volume, tables_y[0]).astype(jnp.bfloat16)
    y_im = (-product("szxy,yk->szxk", reduced_volume, tables_y[1])).astype(jnp.bfloat16)
    x_re = (
        product("szxk,xj->szjk", y_re, tables_x[0]) + product("szxk,xj->szjk", y_im, tables_x[1])
    ).astype(jnp.bfloat16)
    x_im = (
        product("szxk,xj->szjk", y_im, tables_x[0]) - product("szxk,xj->szjk", y_re, tables_x[1])
    ).astype(jnp.bfloat16)
    kx_part = GX // lax.axis_size("zslab")
    re_in = lax.all_to_all(x_re, "zslab", split_axis=2, concat_axis=1, tiled=True)
    im_in = lax.all_to_all(x_im, "zslab", split_axis=2, concat_axis=1, tiled=True)
    out_re = (
        product("szjk,zm->msjk", re_in, tables_z[0]) + product("szjk,zm->msjk", im_in, tables_z[1])
    ).astype(jnp.bfloat16)
    out_im = (
        product("szjk,zm->msjk", im_in, tables_z[0]) - product("szjk,zm->msjk", re_in, tables_z[1])
    ).astype(jnp.bfloat16)
    tile_count = lax.axis_size("tile")
    kz_part = GZ // tile_count
    spectra = (
        lax.all_to_all(out_re, "tile", split_axis=0, concat_axis=0, tiled=True),
        lax.all_to_all(out_im, "tile", split_axis=0, concat_axis=0, tiled=True),
    )
    owner_re = spectra[0].reshape(tile_count, kz_part, slots, kx_part, GY)
    owner_im = spectra[1].reshape(tile_count, kz_part, slots, kx_part, GY)
    phase_real_part, phase_im = cross_phase(owner_re, owner_im, pairs, tiles_here)
    returned = (
        lax.all_to_all(phase_real_part, "tile", split_axis=0, concat_axis=1, tiled=True),
        lax.all_to_all(phase_im, "tile", split_axis=0, concat_axis=1, tiled=True),
    )
    w_re, w_im = inverse_z(returned[0], returned[1], tables_z)
    v_re, v_im = inverse_x(
        lax.all_to_all(w_re, "zslab", split_axis=1, concat_axis=2, tiled=True),
        lax.all_to_all(w_im, "zslab", split_axis=1, concat_axis=2, tiled=True),
        tables_x,
    )
    return product("pzxk,ky->pzxy", v_re, tables_y[0]) - product("pzxk,ky->pzxy", v_im, tables_y[1])


HALF = GY // 2
PLANES = 4
VMEM_BYTES = 32 * 1024 * 1024


def host_tables(length):
    indices = np.arange(length, dtype=np.int32)
    modular = indices[:, None] * indices[None, :] % length
    angles = modular.astype(np.float32) * np.float32(2.0 * math.pi / length)
    factor = np.float32(1.0 / math.sqrt(length))
    return (
        (np.cos(angles) * factor).astype(jnp.bfloat16),
        (np.sin(angles) * factor).astype(jnp.bfloat16),
    )


def half_y_table():
    cosine, sine = host_tables(GY)
    imag = -sine[:, :HALF]
    imag[:, 0] = cosine[:, HALF]
    return np.concatenate([cosine[:, :HALF], imag], axis=1)


def paired_y_table():
    table = np.zeros((2 * GY, GY), jnp.bfloat16)
    table[::2] = half_y_table() * np.array(0.5, jnp.bfloat16)
    table[:, [0, HALF]] *= np.array(0.5, jnp.bfloat16)
    return table


def half_y_inverse():
    cosine, sine = host_tables(GY)
    two = np.array(2.0, jnp.bfloat16)
    real = cosine[:HALF, :] * two
    real[0] = cosine[0]
    imag = -sine[:HALF, :] * two
    imag[0] = cosine[HALF]
    return np.concatenate([real, imag], axis=0)


def mirror_order():
    order = [0, GX // 2]
    for j in range(1, GX // 2):
        order += [j, GX - j]
    return order


def complex_blocks(length, sign):
    cosine, sine = (table.astype(np.float32) for table in host_tables(length))
    return np.array([[cosine, -sign * sine], [sign * sine, cosine]])


def forward_x_table():
    table = np.einsum("oijx,az->joaizx", complex_blocks(GX, -1), np.eye(PLANES))[mirror_order()]
    table = table.reshape(2 * GX * PLANES, 2, PLANES, GX)
    woven = table[:, :, :2].transpose(0, 1, 3, 2).reshape(-1, 2, 2 * GX)
    plain = table[:, :, 2:].reshape(-1, 2, (PLANES - 2) * GX)
    table = np.concatenate([woven, plain], axis=2)
    return table.reshape(2 * GX * PLANES, -1).astype(jnp.bfloat16)


def inverse_x_table():
    table = np.einsum("oijx,az->oaxjiz", complex_blocks(GX, 1), np.eye(PLANES))
    return table.reshape(2 * PLANES * GX, -1).astype(jnp.bfloat16)


def z_rows():
    return np.arange(2 * GZ).reshape(2, GZ // PLANES, PLANES).transpose(1, 0, 2).reshape(-1)


def z_tables():
    forward, inverse = (
        complex_blocks(GZ, sign).transpose(0, 2, 1, 3).reshape(2 * GZ, 2 * GZ) for sign in (-1, 1)
    )
    none = np.zeros((2 * GZ, GZ), np.float32)
    forward_last = np.concatenate([none, forward[:, :GZ]], axis=1)
    inverse_last = np.concatenate([none.T, inverse[:GZ]], axis=0)
    order = z_rows()
    return [
        np.ascontiguousarray(table).astype(jnp.bfloat16)
        for table in (
            forward[:, order],
            inverse[order],
            forward_last[:, order],
            inverse_last[order],
        )
    ]


def imaginary_rows(shape):
    return lax.broadcasted_iota(jnp.int32, shape, 0) % (2 * PLANES) >= PLANES


def first_lane(shape):
    return lax.broadcasted_iota(jnp.int32, shape, 1) == 0


def dot(left, right):
    return jnp.dot(left, right, preferred_element_type=jnp.float32)


def analyse_kernel(
    slots, pairs_ref, extents_ref, tile_ref, *rest
):
    band_refs, (wy_ref, wx_ref, out_ref, crop_ref) = rest[:-4], rest[-4:]
    slot = pl.program_id(0)

    @pl.when(slot == 0)
    def _():
        for p in range(pairs_ref.shape[1]):
            for end in (0, 1):
                named = pairs_ref[2 * end, p] * FACES + pairs_ref[2 * end + 1, p] - tile_ref[0] * slots

                @pl.when((named >= 0) & (named < slots))
                def _():
                    crop_ref[named, 0] = extents_ref[0, p]
                    crop_ref[named, 1] = extents_ref[1, p]

    across, along = crop_ref[slot, 0], crop_ref[slot, 1]

    def live(k, rows):
        lane = lax.broadcasted_iota(jnp.int32, rows.shape, 1)
        return jnp.where((rows < across) & (k * 128 + lane < along), 1.0, 0.0).astype(jnp.bfloat16)

    def halves(rows):
        return (rows + pltpu.roll(rows, 127, 1)).astype(jnp.bfloat16)

    raw_row = lax.broadcasted_iota(jnp.int32, (2 * GX, 128), 0)
    pooled_row = lax.broadcasted_iota(jnp.int32, (GX, 128), 0)
    even = raw_row % 2 == 0
    groups = (2 * GX // 8, 8, 128)
    lives = [
        (live(k, raw_row), live(k, 2 * pooled_row), live(k, 2 * pooled_row + 1))
        for k in range(len(band_refs))
    ]
    block = (2 * PLANES, HALF)
    lane0, imaginary = first_lane(block), imaginary_rows(block)
    sign = jnp.where(imaginary, -1.0, 1.0)
    twice = jnp.where(lane0, 2.0, 1.0)

    def row_pairs(ref, z, mask, shift):
        raw = (ref[0, 0, z] * mask).astype(jnp.float32)
        return raw + pltpu.roll(raw.reshape(groups), shift, 1).reshape(raw.shape)

    def woven(z):
        return [
            halves(jnp.where(even, row_pairs(ref, z, mask, 7), row_pairs(ref, z + 1, mask, 1)))
            for ref, (mask, _, _) in zip(band_refs, lives)
        ]

    def plain(z):
        parts = []
        for ref, (_, *masks) in zip(band_refs, lives):
            rows = [
                (ref[0, 0, z, pl.ds(a, GX, stride=2), :] * masks[a]).astype(jnp.float32) for a in (0, 1)
            ]
            parts.append(halves(rows[0] + rows[1]))
        return parts

    def pool(z):
        return [
            jnp.concatenate(parts, axis=1)
            for parts in (woven(z), *(plain(z + k) for k in range(2, PLANES)))
        ]

    zpart = 4 * PLANES
    zrows = band_refs[0].shape[2]
    planes = sum((pool(z) for z in range(0, zrows, PLANES)), [])
    y = dot(jnp.concatenate(planes, axis=0), wy_ref[...]).astype(jnp.bfloat16)
    y = y.reshape(zrows // PLANES, PLANES * GX, GY)

    def store(start, spectra):
        def at(n):
            rows = spectra[2 * PLANES * n : 2 * PLANES * (n + 1)]
            return [rows[:, k : k + HALF] for k in range(0, rows.shape[1], HALF)]

        def put(j, blocks):
            rows = slice(2 * start, 2 * (start + zpart))
            out_ref[j, 0, rows] = jnp.concatenate(blocks, axis=0).astype(jnp.bfloat16)

        put(0, [a * twice for a in at(0)])
        put(GX // 2, [a * twice for a in at(1)])
        for j in range(1, GX // 2):
            here, mirror = at(2 * j), at(2 * j + 1)
            put(j, [jnp.where(lane0, a + sign * b, a) for a, b in zip(here, mirror)])
            put(
                GX - j,
                [
                    jnp.where(lane0, pltpu.roll(a - sign * b, PLANES, 0), b)
                    for a, b in zip(here, mirror)
                ],
            )

    for start in range(0, zrows, zpart):
        units = [
            jnp.concatenate([y[unit, :, :HALF], y[unit, :, HALF:]], axis=0)
            for unit in range(start // PLANES, (start + zpart) // PLANES)
        ]
        store(start, dot(wx_ref[...], jnp.concatenate(units, axis=1)))


def analyse(band, pairs, extents, tile):
    slots, zrows = band.shape[0] * FACES, band.shape[2]
    tables = (paired_y_table(), forward_x_table())
    whole = [pl.BlockSpec(t.shape, lambda i, *_: (0, 0)) for t in tables]
    lane_blocks = 2 * GY // 128
    return pl.pallas_call(
        functools.partial(analyse_kernel, slots),
        grid_spec=pltpu.PrefetchScalarGridSpec(
            num_scalar_prefetch=3,
            grid=(slots,),
            in_specs=[
                pl.BlockSpec(
                    (1, 1, zrows, 2 * GX, 128),
                    lambda i, *_, k=k: (i // FACES, i % FACES, 0, 0, k),
                )
                for k in range(lane_blocks)
            ]
            + whole,
            out_specs=pl.BlockSpec((GX, 1, 2 * zrows, HALF), lambda i, *_: (0, i, 0, 0)),
            scratch_shapes=[pltpu.SMEM((slots, 2), jnp.int32)],
        ),
        out_shape=jax.ShapeDtypeStruct((GX, slots, 2 * zrows, HALF), jnp.bfloat16),
        compiler_params=pltpu.CompilerParams(vmem_limit_bytes=VMEM_BYTES + VMEM_BYTES * 3 // 4),
        name="analyse",
    )(pairs, extents, tile, *[band] * lane_blocks, *(jnp.asarray(t) for t in tables))


def normalised(a_re, a_im, b_re, b_im):
    cross_re = a_re * b_re + a_im * b_im
    cross_im = a_im * b_re - a_re * b_im
    scale = lax.rsqrt(cross_re * cross_re + cross_im * cross_im + 1.0)
    return (cross_re * scale).astype(jnp.bfloat16), (cross_im * scale).astype(jnp.bfloat16)


def correlate_kernel(
    slabs, tiles_here, pairs_ref, place_ref, in_ref, wz_ref, wzi_ref, wz_last_ref, wzi_last_ref, out_ref
):
    total = pairs_ref.shape[1]
    pairs_here = out_ref.shape[1]
    slab_rows = out_ref.shape[2]
    both_real = (place_ref[0] == 0) | (place_ref[0] == GX // 2)
    block = (2 * GZ, HALF)
    shared = first_lane(block) & imaginary_rows(block)

    def load(p, end):
        tile = pairs_ref[2 * end, p]
        row = tile // tiles_here
        pos = tile % tiles_here * FACES + pairs_ref[2 * end + 1, p]
        return jnp.concatenate([in_ref[row * slabs + s, pos] for s in range(slabs)], axis=0)

    def phase_of(table_ref, ends):
        spec = dot(table_ref[...], jnp.concatenate(ends, axis=1))
        spec = spec.astype(jnp.bfloat16).astype(jnp.float32)
        parts = [spec[:GZ], spec[GZ:]]
        phases = []
        for k in range(0, spec.shape[1], 2 * HALF):
            a, b = slice(k, k + HALF), slice(k + HALF, k + 2 * HALF)
            phase = normalised(parts[0][:, a], parts[1][:, a], parts[0][:, b], parts[1][:, b])
            phases.append(jnp.concatenate(phase, axis=0))
        return jnp.concatenate(phases, axis=1)

    def join(special):
        if special:
            keep = jnp.where(shared, 0.0, 1.0).astype(jnp.bfloat16)
            lane = lax.broadcasted_iota(jnp.int32, block, 1)
            lasts = [jnp.zeros(block, jnp.bfloat16)] * 2
            for p in range(total):
                for end in (0, 1):
                    lasts[end] = jnp.where(lane == p, load(p, end)[:, 0:1], lasts[end])
            last = dot(wzi_last_ref[...], phase_of(wz_last_ref, lasts)).astype(jnp.bfloat16)
        group = 16 if total % 16 == 0 else 8
        for p in range(0, total, group):
            ends = [load(q, end) for q in range(p, p + group) for end in (0, 1)]
            if special:
                ends = [end * keep for end in ends]
            w = dot(wzi_ref[...], phase_of(wz_ref, ends)).astype(jnp.bfloat16)
            for k, q in enumerate(range(p, p + group)):
                whole = w[:, k * HALF : (k + 1) * HALF]
                if special:
                    whole = jnp.where(shared, last[:, q : q + 1], whole)
                for s in range(slabs):
                    out_ref[q // pairs_here * slabs + s, q % pairs_here] = whole[
                        s * slab_rows : (s + 1) * slab_rows
                    ]

    @pl.when(both_real)
    def _():
        join(True)

    @pl.when(jnp.logical_not(both_real))
    def _():
        join(False)


def correlate(spread, pairs, place, slabs, tiles_here):
    devices, _, slab_rows, _ = spread.shape
    pairs_here = pairs.shape[1] * slabs // devices
    tables = z_tables()
    vmem = pl.BlockSpec(memory_space=pltpu.VMEM)
    smem = pl.BlockSpec(memory_space=pltpu.SMEM)
    return pl.pallas_call(
        functools.partial(correlate_kernel, slabs, tiles_here),
        in_specs=[smem, smem] + [vmem] * (1 + len(tables)),
        out_specs=vmem,
        out_shape=jax.ShapeDtypeStruct((devices, pairs_here, slab_rows, HALF), jnp.bfloat16),
        compiler_params=pltpu.CompilerParams(vmem_limit_bytes=VMEM_BYTES),
        name="correlate",
    )(pairs, place, spread, *(jnp.asarray(t) for t in tables))


def synthesise_kernel(in_ref, wx_ref, wy_ref, out_ref, maps_ref, sems):
    pairs_here, slab_rows = in_ref.shape[1:3]
    zrows = slab_rows // 2
    units = zrows // PLANES
    block = (slab_rows, HALF)
    lane0, imaginary = first_lane(block), imaginary_rows(block)
    sign = jnp.where(imaginary, -1.0, 1.0)
    groups = (units, 2 * PLANES, HALF)
    zpart = zrows // sems.shape[1]
    rows = PLANES * GX

    def leave(p, part):
        zs = pl.ds(part * zpart, zpart)
        return pltpu.make_async_copy(maps_ref.at[p, zs], out_ref.at[p, zs], sems.at[p, part])

    for p in range(pairs_here):
        blocks = [None] * GX
        for j in (0, GX // 2):
            blocks[j] = in_ref[j, p].astype(jnp.float32)
        for j in range(1, GX // 2):
            here, mirror = in_ref[j, p].astype(jnp.float32), in_ref[GX - j, p].astype(jnp.float32)
            swapped = pltpu.roll(mirror.reshape(groups), PLANES, 1).reshape(block)
            blocks[j] = jnp.where(lane0, here + swapped, here)
            blocks[GX - j] = jnp.where(lane0, sign * (here - swapped), mirror)
        stacked = jnp.concatenate(
            [
                jnp.concatenate([b[u * 2 * PLANES : (u + 1) * 2 * PLANES] for b in blocks], axis=0)
                for u in range(units)
            ],
            axis=1,
        ).astype(jnp.bfloat16)
        v = dot(wx_ref[...], stacked).astype(jnp.bfloat16)
        cells = [
            jnp.concatenate([v[:rows, k : k + HALF], v[rows:, k : k + HALF]], axis=1)
            for k in range(0, units * HALF, HALF)
        ]
        for part in range(sems.shape[1]):
            of = cells[part * zpart // PLANES : (part + 1) * zpart // PLANES]
            maps = dot(jnp.concatenate(of, axis=0), wy_ref[...])
            maps_ref[p, part * zpart : (part + 1) * zpart] = maps.reshape(zpart, GX, GY)
            leave(p, part).start()
    for p in range(pairs_here):
        for part in range(sems.shape[1]):
            leave(p, part).wait()


def synthesise(returned):
    _, pairs_here, slab_rows, _ = returned.shape
    tables = (inverse_x_table(), half_y_inverse())
    shape = (pairs_here, slab_rows // 2, GX, GY)
    vmem = pl.BlockSpec(memory_space=pltpu.VMEM)
    return pl.pallas_call(
        synthesise_kernel,
        in_specs=[vmem] * (1 + len(tables)),
        out_specs=pl.BlockSpec(memory_space=pl.ANY),
        out_shape=jax.ShapeDtypeStruct(shape, jnp.float32),
        scratch_shapes=[
            pltpu.VMEM(shape, jnp.float32),
            pltpu.SemaphoreType.DMA((pairs_here, slab_rows // (8 * PLANES))),
        ],
        compiler_params=pltpu.CompilerParams(vmem_limit_bytes=VMEM_BYTES),
        name="synthesise",
    )(returned, *(jnp.asarray(t) for t in tables))


def shards(band, pairs, extents):
    tiles, slabs = lax.axis_size("tile"), lax.axis_size("zslab")
    zrows = band.shape[2]
    if tiles * slabs != GX or zrows % (4 * PLANES) or pairs.shape[0] % 8 or pairs.shape[0] % tiles:
        return general_shards(band, pairs, extents)
    pairs, extents = pairs.T, extents.T
    tile = lax.axis_index("tile").astype(jnp.int32)
    device = tile * slabs + lax.axis_index("zslab").astype(jnp.int32)
    spectra = analyse(band, pairs, extents, tile[None])
    spread = lax.all_to_all(spectra, ("tile", "zslab"), split_axis=0, concat_axis=0, tiled=True)
    w = correlate(spread, pairs, device[None], slabs, band.shape[0])
    returned = lax.all_to_all(w, ("tile", "zslab"), split_axis=0, concat_axis=0, tiled=True)
    return synthesise(returned)


def solution(mesh):
    placed = (P("tile", None, "zslab", None, None), P(), P())
    return jax.shard_map(
        shards,
        mesh=mesh,
        in_specs=placed,
        out_specs=P("tile", "zslab", None, None),
        check_vma=False,
    )
```

profile of v0, /device:TPU:0, one launch (start us, length us, event | category | flops | bytes accessed | tf_op | source)
XLA Modules:
  0.0 98.6 jit_solution(18369308423938205138)
XLA Ops:
  0.0 8.5 %analyse.1 = bf16[32,4,64,128]{3,2,1,0:T(8,128)(2,1)} custom-call(s32[4,16]{1,0:T(4,128)} %bitcast.4, s32[2,16]{1,0:T(2,128)} %bitcast.6, s32[1]{0:T(128)} %bitcast.3.tile_ref, bf16[1,4,32,64,512]{4,3,2,1,0:T(8,128)(2,1)} %rest_3_.1, bf16[1,4,32,64,512]{4,3,2,1,0:T(8,128)(2,1)} %rest_3_.1, bf16[1,4,32,64,512]{4,3,2,1,0:T(8,128)(2,1)} %rest_3_.1, ...), custom_call_target="tpu_custom_call" | custom-call | tf_op jit(solution)/shard_map/analyse/pallas_call | solution.py:352
  8.5 0.0 copy-start
  8.5 0.0 copy-start.1
  8.5 0.0 copy-start.2
  8.5 0.0 copy-start.3
  8.6 0.0 copy-start.6
  8.6 7.3 %all-to-all-start = ((bf16[32,4,64,128]{3,2,1,0:T(8,128)(2,1)}), bf16[32,4,64,128]{3,2,1,0:T(8,128)(2,1)S(1)}, u32[]{:S(2)}, u32[]{:S(2)}) async-start(bf16[32,4,64,128]{3,2,1,0:T(8,128)(2,1)} %analyse.1), calls=%async_computation | async-start | bytes 4194304 | tf_op jit(solution)/shard_map/all_to_all | solution.py:531
  15.9 48.8 %all-to-all-done.in_ref = bf16[32,4,64,128]{3,2,1,0:T(8,128)(2,1)S(1)} async-done(((bf16[32,4,64,128]{3,2,1,0:T(8,128)(2,1)}), bf16[32,4,64,128]{3,2,1,0:T(8,128)(2,1)S(1)}, u32[]{:S(2)}, u32[]{:S(2)}) %all-to-all-start) | async-done | bytes 2097184 | tf_op jit(solution)/shard_map/all_to_all | solution.py:531
  64.7 0.0 copy-done
  64.7 0.0 copy-done.1
  64.7 0.0 copy-done.2
  64.7 0.0 copy-done.3
  64.7 0.0 copy-done.6
  64.7 0.0 copy-start.4
  64.7 0.0 copy-start.5
  64.7 2.8 %correlate.1 = bf16[32,2,64,128]{3,2,1,0:T(8,128)(2,1)S(1)} custom-call(s32[4,16]{1,0:T(4,128)S(1)} %bitcast.5, s32[1]{0:T(128)} %bitcast.1.place_ref, bf16[32,4,64,128]{3,2,1,0:T(8,128)(2,1)S(1)} %all-to-all-done.in_ref, bf16[256,256]{1,0:T(8,128)(2,1)S(1)} %copy-done.3, bf16[256,256]{1,0:T(8,128)(2,1)S(1)} %copy-done.2, bf16[256,256]{1,0:T(8,128)(2,1)S(1)} %copy-done.1, ...), custom_call_target="tpu_custom_call" | custom-call | tf_op jit(solution)/shard_map/correlate/pallas_call | solution.py:447
  67.5 29.3 %all_to_all.10.in_ref = bf16[32,2,64,128]{3,2,1,0:T(8,128)(2,1)S(1)} all-to-all(bf16[32,2,64,128]{3,2,1,0:T(8,128)(2,1)S(1)} %correlate.1), channel_id=1, replica_groups=mesh['tile'=8,'zslab'=4] {'tile','zslab'}, dimensions={0} | all-to-all | bytes 2097152 | tf_op jit(solution)/shard_map/all_to_all | solution.py:533
  96.8 0.0 copy-done.4
  96.8 0.0 copy-done.5
  96.8 1.8 %synthesise.1 = f32[2,32,32,256]{3,2,1,0:T(8,128)} custom-call(bf16[32,2,64,128]{3,2,1,0:T(8,128)(2,1)S(1)} %all_to_all.10.in_ref, bf16[256,256]{1,0:T(8,128)(2,1)S(1)} %copy-done.5, bf16[256,256]{1,0:T(8,128)(2,1)S(1)} %copy-done.4), custom_call_target="tpu_custom_call" | custom-call | tf_op jit(solution)/shard_map/synthesise/pallas_call | solution.py:508
Async XLA Ops:
  8.5 56.1 %copy-start = (bf16[256,256]{1,0:T(8,128)(2,1)S(1)}, bf16[256,256]{1,0:T(8,128)(2,1)}, u32[]{:S(2)}) copy-start(bf16[256,256]{1,0:T(8,128)(2,1)} %constant.32.clone.wzi_last_ref) | copy-start | bytes 393220
  8.5 56.1 %copy-start.1 = (bf16[256,256]{1,0:T(8,128)(2,1)S(1)}, bf16[256,256]{1,0:T(8,128)(2,1)}, u32[]{:S(2)}) copy-start(bf16[256,256]{1,0:T(8,128)(2,1)} %constant.31.clone.wz_last_ref) | copy-start | bytes 393220
  8.5 56.1 %copy-start.2 = (bf16[256,256]{1,0:T(8,128)(2,1)S(1)}, bf16[256,256]{1,0:T(8,128)(2,1)}, u32[]{:S(2)}) copy-start(bf16[256,256]{1,0:T(8,128)(2,1)} %constant.30.clone.wzi_ref) | copy-start | bytes 393220
  8.5 56.1 %copy-start.3 = (bf16[256,256]{1,0:T(8,128)(2,1)S(1)}, bf16[256,256]{1,0:T(8,128)(2,1)}, u32[]{:S(2)}) copy-start(bf16[256,256]{1,0:T(8,128)(2,1)} %constant.29.clone.wz_ref) | copy-start | bytes 393220
  8.6 56.1 %copy-start.6 = (s32[16,4]{0,1:T(4,128)S(1)}, s32[16,4]{0,1:T(4,128)}, u32[]{:S(2)}) copy-start(s32[16,4]{0,1:T(4,128)} %param.12) | copy-start | bytes 772
  8.6 56.1 %all-to-all-start = ((bf16[32,4,64,128]{3,2,1,0:T(8,128)(2,1)}), bf16[32,4,64,128]{3,2,1,0:T(8,128)(2,1)S(1)}, u32[]{:S(2)}, u32[]{:S(2)}) async-start(bf16[32,4,64,128]{3,2,1,0:T(8,128)(2,1)} %analyse.1), calls=%async_computation | async-start | bytes 4194304 | tf_op jit(solution)/shard_map/all_to_all | solution.py:531
  64.7 32.1 %copy-start.4 = (bf16[256,256]{1,0:T(8,128)(2,1)S(1)}, bf16[256,256]{1,0:T(8,128)(2,1)}, u32[]{:S(2)}) copy-start(bf16[256,256]{1,0:T(8,128)(2,1)} %constant.34.clone.wy_ref) | copy-start | bytes 393220
  64.7 32.1 %copy-start.5 = (bf16[256,256]{1,0:T(8,128)(2,1)S(1)}, bf16[256,256]{1,0:T(8,128)(2,1)}, u32[]{:S(2)}) copy-start(bf16[256,256]{1,0:T(8,128)(2,1)} %constant.33.clone.wx_ref) | copy-start | bytes 393220
where the time goes:
time: 98.9 us; the launch traced here: 98.6 us
  waiting for transfers between devices  48.8 us (49%)
  blocking collectives  29.3 us (30%)
  Pallas kernels  13.2 us (13%)
  starting transfers between devices  7.3 us (7%)
    all_to_all x1, waiting for transfers between devices, shards(): lax.all_to_all(spectra, ('tile', 'zslab'), split_axis=0, concat_axis=0, t...  48.8 us
    all_to_all x1, blocking collectives, shards(): lax.all_to_all(w, ('tile', 'zslab'), split_axis=0, concat_axis=0, tiled=T...  29.3 us
    pallas_call x1, Pallas kernels, analyse(): pl.pallas_call(functools.partial(analyse_kernel, slots), grid_spec=pltpu....  8.53 us
    all_to_all x1, starting transfers between devices, shards(): lax.all_to_all(spectra, ('tile', 'zslab'), split_axis=0, concat_axis=0, t...  7.3 us
    pallas_call x1, Pallas kernels, correlate(): pl.pallas_call(functools.partial(correlate_kernel, slabs, tiles_here), in...  2.81 us
  transfers between devices with their start and end apart: 1, of which 1 were waited for; matrix products, arithmetic and copies ran while one was open for 0% of the time, Pallas kernels for 0%

commit v1 on v0

--- a/solution.py
+++ b/solution.py
@@ -379,8 +379,14 @@
 
 
 def correlate_kernel(
-    slabs, tiles_here, pairs_ref, place_ref, in_ref, wz_ref, wzi_ref, wz_last_ref, wzi_last_ref, out_ref
+    sizes, tiles_here, pairs_ref, place_ref, in_ref, wz_ref, wzi_ref, wz_last_ref, wzi_last_ref, out_ref
 ):
+    x, y, cores = sizes
+    slabs = y * cores
+
+    def place_of(owner, s):
+        return owner // x * (y * x * cores) + owner % x * cores + s // cores * (x * cores) + s % cores
+
     total = pairs_ref.shape[1]
     pairs_here = out_ref.shape[1]
     slab_rows = out_ref.shape[2]
@@ -392,7 +398,7 @@
         tile = pairs_ref[2 * end, p]
         row = tile // tiles_here
         pos = tile % tiles_here * FACES + pairs_ref[2 * end + 1, p]
-        return jnp.concatenate([in_ref[row * slabs + s, pos] for s in range(slabs)], axis=0)
+        return jnp.concatenate([in_ref[place_of(row, s), pos] for s in range(slabs)], axis=0)
 
     def phase_of(table_ref, ends):
         spec = dot(table_ref[...], jnp.concatenate(ends, axis=1))
@@ -425,7 +431,7 @@
                 if special:
                     whole = jnp.where(shared, last[:, q : q + 1], whole)
                 for s in range(slabs):
-                    out_ref[q // pairs_here * slabs + s, q % pairs_here] = whole[
+                    out_ref[place_of(q // pairs_here, s), q % pairs_here] = whole[
                         s * slab_rows : (s + 1) * slab_rows
                     ]
 
@@ -438,14 +444,14 @@
         join(False)
 
 
-def correlate(spread, pairs, place, slabs, tiles_here):
+def correlate(spread, pairs, place, sizes, tiles_here):
     devices, _, slab_rows, _ = spread.shape
-    pairs_here = pairs.shape[1] * slabs // devices
+    pairs_here = pairs.shape[1] * sizes[1] * sizes[2] // devices
     tables = z_tables()
     vmem = pl.BlockSpec(memory_space=pltpu.VMEM)
     smem = pl.BlockSpec(memory_space=pltpu.SMEM)
     return pl.pallas_call(
-        functools.partial(correlate_kernel, slabs, tiles_here),
+        functools.partial(correlate_kernel, sizes, tiles_here),
         in_specs=[smem, smem] + [vmem] * (1 + len(tables)),
         out_specs=vmem,
         out_shape=jax.ShapeDtypeStruct((devices, pairs_here, slab_rows, HALF), jnp.bfloat16),
@@ -519,27 +525,36 @@
     )(returned, *(jnp.asarray(t) for t in tables))
 
 
-def shards(band, pairs, extents):
-    tiles, slabs = lax.axis_size("tile"), lax.axis_size("zslab")
-    zrows = band.shape[2]
-    if tiles * slabs != GX or zrows % (4 * PLANES) or pairs.shape[0] % 8 or pairs.shape[0] % tiles:
-        return general_shards(band, pairs, extents)
+ORDER = ("z", "y", "x", "core")
+
+
+def placed_shards(band, pairs, extents):
+    x, y, cores = (lax.axis_size(axis) for axis in ("x", "y", "core"))
     pairs, extents = pairs.T, extents.T
-    tile = lax.axis_index("tile").astype(jnp.int32)
-    device = tile * slabs + lax.axis_index("zslab").astype(jnp.int32)
+    tile = (lax.axis_index("z") * x + lax.axis_index("x")).astype(jnp.int32)
+    device = lax.axis_index(ORDER).astype(jnp.int32)
     spectra = analyse(band, pairs, extents, tile[None])
-    spread = lax.all_to_all(spectra, ("tile", "zslab"), split_axis=0, concat_axis=0, tiled=True)
-    w = correlate(spread, pairs, device[None], slabs, band.shape[0])
-    returned = lax.all_to_all(w, ("tile", "zslab"), split_axis=0, concat_axis=0, tiled=True)
+    spread = lax.all_to_all(spectra, ORDER, split_axis=0, concat_axis=0, tiled=True)
+    w = correlate(spread, pairs, device[None], (x, y, cores), band.shape[0])
+    returned = lax.all_to_all(w, ORDER, split_axis=0, concat_axis=0, tiled=True)
     return synthesise(returned)
 
 
 def solution(mesh):
-    placed = (P("tile", None, "zslab", None, None), P(), P())
+    tiles, slabs = mesh.devices.shape
+    cores = 2
+    side = max(slabs // cores, 1)
+    if tiles * slabs == GX and slabs % cores == 0 and tiles % side == 0:
+        over = jax.sharding.Mesh(
+            mesh.devices.reshape(tiles // side, side, slabs // cores, cores), ("z", "x", "y", "core")
+        )
+        tile, slab, body = ("z", "x"), ("y", "core"), placed_shards
+    else:
+        over, tile, slab, body = mesh, "tile", "zslab", general_shards
     return jax.shard_map(
-        shards,
-        mesh=mesh,
-        in_specs=placed,
-        out_specs=P("tile", "zslab", None, None),
+        body,
+        mesh=over,
+        in_specs=(P(tile, None, slab, None, None), P(), P()),
+        out_specs=P(tile, slab, None, None),
         check_vma=False,
     )

time: 98.9 us -> 99 us (level)
  no operation moved by 1% of the time
where the time goes in v1:
time: 99 us; the launch traced here: 98.7 us
  waiting for transfers between devices  48.9 us (49%)
  blocking collectives  29.1 us (29%)
  Pallas kernels  13.2 us (13%)
  starting transfers between devices  7.3 us (7%)
    all_to_all x1, waiting for transfers between devices, placed_shards(): lax.all_to_all(spectra, ORDER, split_axis=0, concat_axis=0, tiled=True)  48.9 us
    all_to_all x1, blocking collectives, placed_shards(): returned = lax.all_to_all(w, ORDER, split_axis=0, concat_axis=0, tiled=True)  29.1 us
    pallas_call x1, Pallas kernels, analyse(): pl.pallas_call(functools.partial(analyse_kernel, slots), grid_spec=pltpu....  8.53 us
    all_to_all x1, starting transfers between devices, placed_shards(): lax.all_to_all(spectra, ORDER, split_axis=0, concat_axis=0, tiled=True)  7.3 us
    pallas_call x1, Pallas kernels, correlate(): pl.pallas_call(functools.partial(correlate_kernel, sizes, tiles_here), in...  2.87 us
  transfers between devices with their start and end apart: 1, of which 1 were waited for; matrix products, arithmetic and copies ran while one was open for 0% of the time, Pallas kernels for 0%

profile of v1, /device:TPU:0, one launch (start us, length us, event | category | flops | bytes accessed | tf_op | source)
XLA Modules:
  0.0 98.7 jit_solution(9181351650298696375)
XLA Ops:
  0.0 8.5 %analyse.1 = bf16[32,4,64,128]{3,2,1,0:T(8,128)(2,1)} custom-call(s32[4,16]{1,0:T(4,128)} %bitcast.4, s32[2,16]{1,0:T(2,128)} %bitcast.6, s32[1]{0:T(128)} %bitcast.3.tile_ref, bf16[1,4,32,64,512]{4,3,2,1,0:T(8,128)(2,1)} %rest_3_.1, bf16[1,4,32,64,512]{4,3,2,1,0:T(8,128)(2,1)} %rest_3_.1, bf16[1,4,32,64,512]{4,3,2,1,0:T(8,128)(2,1)} %rest_3_.1, ...), custom_call_target="tpu_custom_call" | custom-call | tf_op jit(solution)/shard_map/analyse/pallas_call | solution.py:352
  8.5 0.0 copy-start
  8.5 0.0 copy-start.1
  8.5 0.0 copy-start.2
  8.5 0.0 copy-start.3
  8.6 0.0 copy-start.6
  8.6 7.3 %all-to-all-start = ((bf16[32,4,64,128]{3,2,1,0:T(8,128)(2,1)}), bf16[32,4,64,128]{3,2,1,0:T(8,128)(2,1)S(1)}, u32[]{:S(2)}, u32[]{:S(2)}) async-start(bf16[32,4,64,128]{3,2,1,0:T(8,128)(2,1)} %analyse.1), calls=%async_computation | async-start | bytes 4194304 | tf_op jit(solution)/shard_map/all_to_all | solution.py:537
  15.9 48.9 %all-to-all-done.in_ref = bf16[32,4,64,128]{3,2,1,0:T(8,128)(2,1)S(1)} async-done(((bf16[32,4,64,128]{3,2,1,0:T(8,128)(2,1)}), bf16[32,4,64,128]{3,2,1,0:T(8,128)(2,1)S(1)}, u32[]{:S(2)}, u32[]{:S(2)}) %all-to-all-start) | async-done | bytes 2097184 | tf_op jit(solution)/shard_map/all_to_all | solution.py:537
  64.8 0.0 copy-done
  64.8 0.0 copy-done.1
  64.8 0.0 copy-done.2
  64.8 0.0 copy-done.3
  64.8 0.0 copy-done.6
  64.8 0.0 copy-start.4
  64.8 0.0 copy-start.5
  64.8 2.9 %correlate.1 = bf16[32,2,64,128]{3,2,1,0:T(8,128)(2,1)S(1)} custom-call(s32[4,16]{1,0:T(4,128)S(1)} %bitcast.5, s32[1]{0:T(128)} %bitcast.1.place_ref, bf16[32,4,64,128]{3,2,1,0:T(8,128)(2,1)S(1)} %all-to-all-done.in_ref, bf16[256,256]{1,0:T(8,128)(2,1)S(1)} %copy-done.3, bf16[256,256]{1,0:T(8,128)(2,1)S(1)} %copy-done.2, bf16[256,256]{1,0:T(8,128)(2,1)S(1)} %copy-done.1, ...), custom_call_target="tpu_custom_call" | custom-call | tf_op jit(solution)/shard_map/correlate/pallas_call | solution.py:453
  67.7 29.1 %all_to_all.10.in_ref = bf16[32,2,64,128]{3,2,1,0:T(8,128)(2,1)S(1)} all-to-all(bf16[32,2,64,128]{3,2,1,0:T(8,128)(2,1)S(1)} %correlate.1), channel_id=1, replica_groups=mesh['z'=4,'x'=2,'y'=2,'core'=2] {'z','y','x','core'}, dimensions={0} | all-to-all | bytes 2097152 | tf_op jit(solution)/shard_map/all_to_all | solution.py:539
  96.8 0.0 copy-done.4
  96.9 0.0 copy-done.5
  96.9 1.8 %synthesise.1 = f32[2,32,32,256]{3,2,1,0:T(8,128)} custom-call(bf16[32,2,64,128]{3,2,1,0:T(8,128)(2,1)S(1)} %all_to_all.10.in_ref, bf16[256,256]{1,0:T(8,128)(2,1)S(1)} %copy-done.5, bf16[256,256]{1,0:T(8,128)(2,1)S(1)} %copy-done.4), custom_call_target="tpu_custom_call" | custom-call | tf_op jit(solution)/shard_map/synthesise/pallas_call | solution.py:514
Async XLA Ops:
  8.5 56.3 %copy-start = (bf16[256,256]{1,0:T(8,128)(2,1)S(1)}, bf16[256,256]{1,0:T(8,128)(2,1)}, u32[]{:S(2)}) copy-start(bf16[256,256]{1,0:T(8,128)(2,1)} %constant.41.clone.wzi_last_ref) | copy-start | bytes 393220
  8.5 56.3 %copy-start.1 = (bf16[256,256]{1,0:T(8,128)(2,1)S(1)}, bf16[256,256]{1,0:T(8,128)(2,1)}, u32[]{:S(2)}) copy-start(bf16[256,256]{1,0:T(8,128)(2,1)} %constant.40.clone.wz_last_ref) | copy-start | bytes 393220
  8.5 56.3 %copy-start.2 = (bf16[256,256]{1,0:T(8,128)(2,1)S(1)}, bf16[256,256]{1,0:T(8,128)(2,1)}, u32[]{:S(2)}) copy-start(bf16[256,256]{1,0:T(8,128)(2,1)} %constant.39.clone.wzi_ref) | copy-start | bytes 393220
  8.5 56.2 %copy-start.3 = (bf16[256,256]{1,0:T(8,128)(2,1)S(1)}, bf16[256,256]{1,0:T(8,128)(2,1)}, u32[]{:S(2)}) copy-start(bf16[256,256]{1,0:T(8,128)(2,1)} %constant.38.clone.wz_ref) | copy-start | bytes 393220
  8.6 56.2 %copy-start.6 = (s32[16,4]{0,1:T(4,128)S(1)}, s32[16,4]{0,1:T(4,128)}, u32[]{:S(2)}) copy-start(s32[16,4]{0,1:T(4,128)} %param.12) | copy-start | bytes 772
  8.6 56.2 %all-to-all-start = ((bf16[32,4,64,128]{3,2,1,0:T(8,128)(2,1)}), bf16[32,4,64,128]{3,2,1,0:T(8,128)(2,1)S(1)}, u32[]{:S(2)}, u32[]{:S(2)}) async-start(bf16[32,4,64,128]{3,2,1,0:T(8,128)(2,1)} %analyse.1), calls=%async_computation | async-start | bytes 4194304 | tf_op jit(solution)/shard_map/all_to_all | solution.py:537
  64.8 32.0 %copy-start.4 = (bf16[256,256]{1,0:T(8,128)(2,1)S(1)}, bf16[256,256]{1,0:T(8,128)(2,1)}, u32[]{:S(2)}) copy-start(bf16[256,256]{1,0:T(8,128)(2,1)} %constant.43.clone.wy_ref) | copy-start | bytes 393220
  64.8 32.0 %copy-start.5 = (bf16[256,256]{1,0:T(8,128)(2,1)S(1)}, bf16[256,256]{1,0:T(8,128)(2,1)}, u32[]{:S(2)}) copy-start(bf16[256,256]{1,0:T(8,128)(2,1)} %constant.42.clone.wx_ref) | copy-start | bytes 393220

commit v2 on v1

--- a/solution.py
+++ b/solution.py
@@ -385,7 +385,7 @@
     slabs = y * cores
 
     def place_of(owner, s):
-        return owner // x * (y * x * cores) + owner % x * cores + s // cores * (x * cores) + s % cores
+        return owner // x * (cores * x * y) + s % cores * (x * y) + owner % x * y + s // cores
 
     total = pairs_ref.shape[1]
     pairs_here = out_ref.shape[1]
@@ -525,7 +525,7 @@
     )(returned, *(jnp.asarray(t) for t in tables))
 
 
-ORDER = ("z", "y", "x", "core")
+ORDER = ("z", "core", "x", "y")
 
 
 def placed_shards(band, pairs, extents):

time: 99 us -> 98.6 us (level)
  no operation moved by 1% of the time
where the time goes in v2:
time: 98.6 us; the launch traced here: 98.3 us
  waiting for transfers between devices  48.7 us (49%)
  blocking collectives  29 us (29%)
  Pallas kernels  13.2 us (13%)
  starting transfers between devices  7.3 us (7%)
    all_to_all x1, waiting for transfers between devices, placed_shards(): lax.all_to_all(spectra, ORDER, split_axis=0, concat_axis=0, tiled=True)  48.7 us
    all_to_all x1, blocking collectives, placed_shards(): returned = lax.all_to_all(w, ORDER, split_axis=0, concat_axis=0, tiled=True)  29 us
    pallas_call x1, Pallas kernels, analyse(): pl.pallas_call(functools.partial(analyse_kernel, slots), grid_spec=pltpu....  8.53 us
    all_to_all x1, starting transfers between devices, placed_shards(): lax.all_to_all(spectra, ORDER, split_axis=0, concat_axis=0, tiled=True)  7.3 us
    pallas_call x1, Pallas kernels, correlate(): pl.pallas_call(functools.partial(correlate_kernel, sizes, tiles_here), in...  2.87 us
  transfers between devices with their start and end apart: 1, of which 1 were waited for; matrix products, arithmetic and copies ran while one was open for 0% of the time, Pallas kernels for 0%

profile of v2, /device:TPU:0, one launch (start us, length us, event | category | flops | bytes accessed | tf_op | source)
XLA Modules:
  0.0 98.3 jit_solution(4553950728266024335)
XLA Ops:
  0.0 8.5 %analyse.1 = bf16[32,4,64,128]{3,2,1,0:T(8,128)(2,1)} custom-call(s32[4,16]{1,0:T(4,128)} %bitcast.4, s32[2,16]{1,0:T(2,128)} %bitcast.6, s32[1]{0:T(128)} %bitcast.3.tile_ref, bf16[1,4,32,64,512]{4,3,2,1,0:T(8,128)(2,1)} %rest_3_.1, bf16[1,4,32,64,512]{4,3,2,1,0:T(8,128)(2,1)} %rest_3_.1, bf16[1,4,32,64,512]{4,3,2,1,0:T(8,128)(2,1)} %rest_3_.1, ...), custom_call_target="tpu_custom_call" | custom-call | tf_op jit(solution)/shard_map/analyse/pallas_call | solution.py:352
  8.5 0.0 copy-start
  8.5 0.0 copy-start.1
  8.5 0.0 copy-start.2
  8.5 0.0 copy-start.3
  8.6 0.0 copy-start.6
  8.6 7.3 %all-to-all-start = ((bf16[32,4,64,128]{3,2,1,0:T(8,128)(2,1)}), bf16[32,4,64,128]{3,2,1,0:T(8,128)(2,1)S(1)}, u32[]{:S(2)}, u32[]{:S(2)}) async-start(bf16[32,4,64,128]{3,2,1,0:T(8,128)(2,1)} %analyse.1), calls=%async_computation | async-start | bytes 4194304 | tf_op jit(solution)/shard_map/all_to_all | solution.py:537
  15.9 48.7 %all-to-all-done.in_ref = bf16[32,4,64,128]{3,2,1,0:T(8,128)(2,1)S(1)} async-done(((bf16[32,4,64,128]{3,2,1,0:T(8,128)(2,1)}), bf16[32,4,64,128]{3,2,1,0:T(8,128)(2,1)S(1)}, u32[]{:S(2)}, u32[]{:S(2)}) %all-to-all-start) | async-done | bytes 2097184 | tf_op jit(solution)/shard_map/all_to_all | solution.py:537
  64.6 0.0 copy-done
  64.6 0.0 copy-done.1
  64.6 0.0 copy-done.2
  64.6 0.0 copy-done.3
  64.6 0.0 copy-done.6
  64.6 0.0 copy-start.4
  64.6 0.0 copy-start.5
  64.6 2.9 %correlate.1 = bf16[32,2,64,128]{3,2,1,0:T(8,128)(2,1)S(1)} custom-call(s32[4,16]{1,0:T(4,128)S(1)} %bitcast.5, s32[1]{0:T(128)} %bitcast.1.place_ref, bf16[32,4,64,128]{3,2,1,0:T(8,128)(2,1)S(1)} %all-to-all-done.in_ref, bf16[256,256]{1,0:T(8,128)(2,1)S(1)} %copy-done.3, bf16[256,256]{1,0:T(8,128)(2,1)S(1)} %copy-done.2, bf16[256,256]{1,0:T(8,128)(2,1)S(1)} %copy-done.1, ...), custom_call_target="tpu_custom_call" | custom-call | tf_op jit(solution)/shard_map/correlate/pallas_call | solution.py:453
  67.5 29.0 %all_to_all.10.in_ref = bf16[32,2,64,128]{3,2,1,0:T(8,128)(2,1)S(1)} all-to-all(bf16[32,2,64,128]{3,2,1,0:T(8,128)(2,1)S(1)} %correlate.1), channel_id=1, replica_groups=mesh['z'=4,'x'=2,'y'=2,'core'=2] {'z','core','x','y'}, dimensions={0} | all-to-all | bytes 2097152 | tf_op jit(solution)/shard_map/all_to_all | solution.py:539
  96.5 0.0 copy-done.4
  96.5 0.0 copy-done.5
  96.5 1.8 %synthesise.1 = f32[2,32,32,256]{3,2,1,0:T(8,128)} custom-call(bf16[32,2,64,128]{3,2,1,0:T(8,128)(2,1)S(1)} %all_to_all.10.in_ref, bf16[256,256]{1,0:T(8,128)(2,1)S(1)} %copy-done.5, bf16[256,256]{1,0:T(8,128)(2,1)S(1)} %copy-done.4), custom_call_target="tpu_custom_call" | custom-call | tf_op jit(solution)/shard_map/synthesise/pallas_call | solution.py:514
Async XLA Ops:
  8.5 56.1 %copy-start = (bf16[256,256]{1,0:T(8,128)(2,1)S(1)}, bf16[256,256]{1,0:T(8,128)(2,1)}, u32[]{:S(2)}) copy-start(bf16[256,256]{1,0:T(8,128)(2,1)} %constant.41.clone.wzi_last_ref) | copy-start | bytes 393220
  8.5 56.1 %copy-start.1 = (bf16[256,256]{1,0:T(8,128)(2,1)S(1)}, bf16[256,256]{1,0:T(8,128)(2,1)}, u32[]{:S(2)}) copy-start(bf16[256,256]{1,0:T(8,128)(2,1)} %constant.40.clone.wz_last_ref) | copy-start | bytes 393220
  8.5 56.1 %copy-start.2 = (bf16[256,256]{1,0:T(8,128)(2,1)S(1)}, bf16[256,256]{1,0:T(8,128)(2,1)}, u32[]{:S(2)}) copy-start(bf16[256,256]{1,0:T(8,128)(2,1)} %constant.39.clone.wzi_ref) | copy-start | bytes 393220
  8.5 56.1 %copy-start.3 = (bf16[256,256]{1,0:T(8,128)(2,1)S(1)}, bf16[256,256]{1,0:T(8,128)(2,1)}, u32[]{:S(2)}) copy-start(bf16[256,256]{1,0:T(8,128)(2,1)} %constant.38.clone.wz_ref) | copy-start | bytes 393220
  8.6 56.1 %copy-start.6 = (s32[16,4]{0,1:T(4,128)S(1)}, s32[16,4]{0,1:T(4,128)}, u32[]{:S(2)}) copy-start(s32[16,4]{0,1:T(4,128)} %param.12) | copy-start | bytes 772
  8.6 56.0 %all-to-all-start = ((bf16[32,4,64,128]{3,2,1,0:T(8,128)(2,1)}), bf16[32,4,64,128]{3,2,1,0:T(8,128)(2,1)S(1)}, u32[]{:S(2)}, u32[]{:S(2)}) async-start(bf16[32,4,64,128]{3,2,1,0:T(8,128)(2,1)} %analyse.1), calls=%async_computation | async-start | bytes 4194304 | tf_op jit(solution)/shard_map/all_to_all | solution.py:537
  64.6 31.9 %copy-start.4 = (bf16[256,256]{1,0:T(8,128)(2,1)S(1)}, bf16[256,256]{1,0:T(8,128)(2,1)}, u32[]{:S(2)}) copy-start(bf16[256,256]{1,0:T(8,128)(2,1)} %constant.43.clone.wy_ref) | copy-start | bytes 393220
  64.6 31.9 %copy-start.5 = (bf16[256,256]{1,0:T(8,128)(2,1)S(1)}, bf16[256,256]{1,0:T(8,128)(2,1)}, u32[]{:S(2)}) copy-start(bf16[256,256]{1,0:T(8,128)(2,1)} %constant.42.clone.wx_ref) | copy-start | bytes 393220

commit v3 on v2

--- a/solution.py
+++ b/solution.py
@@ -475,6 +475,7 @@
         zs = pl.ds(part * zpart, zpart)
         return pltpu.make_async_copy(maps_ref.at[p, zs], out_ref.at[p, zs], sems.at[p, part])
 
+    stacks = []
     for p in range(pairs_here):
         blocks = [None] * GX
         for j in (0, GX // 2):
@@ -491,7 +492,10 @@
             ],
             axis=1,
         ).astype(jnp.bfloat16)
-        v = dot(wx_ref[...], stacked).astype(jnp.bfloat16)
+        stacks.append(stacked)
+    both = dot(wx_ref[...], jnp.concatenate(stacks, axis=1)).astype(jnp.bfloat16)
+    for p in range(pairs_here):
+        v = both[:, p * units * HALF : (p + 1) * units * HALF]
         cells = [
             jnp.concatenate([v[:rows, k : k + HALF], v[rows:, k : k + HALF]], axis=1)
             for k in range(0, units * HALF, HALF)

time: 98.6 us -> 98.9 us (level)
  no operation moved by 1% of the time
where the time goes in v3:
time: 98.9 us; the launch traced here: 98.6 us
  waiting for transfers between devices  48.7 us (49%)
  blocking collectives  29 us (29%)
  Pallas kernels  13.5 us (14%)
  starting transfers between devices  7.3 us (7%)
    all_to_all x1, waiting for transfers between devices, placed_shards(): lax.all_to_all(spectra, ORDER, split_axis=0, concat_axis=0, tiled=True)  48.7 us
    all_to_all x1, blocking collectives, placed_shards(): returned = lax.all_to_all(w, ORDER, split_axis=0, concat_axis=0, tiled=True)  29 us
    pallas_call x1, Pallas kernels, analyse(): pl.pallas_call(functools.partial(analyse_kernel, slots), grid_spec=pltpu....  8.53 us
    all_to_all x1, starting transfers between devices, placed_shards(): lax.all_to_all(spectra, ORDER, split_axis=0, concat_axis=0, tiled=True)  7.3 us
    pallas_call x1, Pallas kernels, correlate(): pl.pallas_call(functools.partial(correlate_kernel, sizes, tiles_here), in...  2.87 us
    pallas_call x1, Pallas kernels, synthesise(): pl.pallas_call(synthesise_kernel, in_specs=[vmem] * (1 + len(tables)), ou...  2.09 us
  transfers between devices with their start and end apart: 1, of which 1 were waited for; matrix products, arithmetic and copies ran while one was open for 0% of the time, Pallas kernels for 0%

profile of v3, /device:TPU:0, one launch (start us, length us, event | category | flops | bytes accessed | tf_op | source)
XLA Modules:
  0.0 98.6 jit_solution(6251767757525581650)
XLA Ops:
  0.0 8.5 %analyse.1 = bf16[32,4,64,128]{3,2,1,0:T(8,128)(2,1)} custom-call(s32[4,16]{1,0:T(4,128)} %bitcast.4, s32[2,16]{1,0:T(2,128)} %bitcast.6, s32[1]{0:T(128)} %bitcast.3.tile_ref, bf16[1,4,32,64,512]{4,3,2,1,0:T(8,128)(2,1)} %rest_3_.1, bf16[1,4,32,64,512]{4,3,2,1,0:T(8,128)(2,1)} %rest_3_.1, bf16[1,4,32,64,512]{4,3,2,1,0:T(8,128)(2,1)} %rest_3_.1, ...), custom_call_target="tpu_custom_call" | custom-call | tf_op jit(solution)/shard_map/analyse/pallas_call | solution.py:352
  8.5 0.0 copy-start
  8.5 0.0 copy-start.1
  8.5 0.0 copy-start.2
  8.5 0.0 copy-start.3
  8.6 0.0 copy-start.6
  8.6 7.3 %all-to-all-start = ((bf16[32,4,64,128]{3,2,1,0:T(8,128)(2,1)}), bf16[32,4,64,128]{3,2,1,0:T(8,128)(2,1)S(1)}, u32[]{:S(2)}, u32[]{:S(2)}) async-start(bf16[32,4,64,128]{3,2,1,0:T(8,128)(2,1)} %analyse.1), calls=%async_computation | async-start | bytes 4194304 | tf_op jit(solution)/shard_map/all_to_all | solution.py:541
  15.9 48.7 %all-to-all-done.in_ref = bf16[32,4,64,128]{3,2,1,0:T(8,128)(2,1)S(1)} async-done(((bf16[32,4,64,128]{3,2,1,0:T(8,128)(2,1)}), bf16[32,4,64,128]{3,2,1,0:T(8,128)(2,1)S(1)}, u32[]{:S(2)}, u32[]{:S(2)}) %all-to-all-start) | async-done | bytes 2097184 | tf_op jit(solution)/shard_map/all_to_all | solution.py:541
  64.6 0.0 copy-done
  64.6 0.0 copy-done.1
  64.6 0.0 copy-done.2
  64.6 0.0 copy-done.3
  64.6 0.0 copy-done.6
  64.6 0.0 copy-start.4
  64.6 0.0 copy-start.5
  64.6 2.9 %correlate.1 = bf16[32,2,64,128]{3,2,1,0:T(8,128)(2,1)S(1)} custom-call(s32[4,16]{1,0:T(4,128)S(1)} %bitcast.5, s32[1]{0:T(128)} %bitcast.1.place_ref, bf16[32,4,64,128]{3,2,1,0:T(8,128)(2,1)S(1)} %all-to-all-done.in_ref, bf16[256,256]{1,0:T(8,128)(2,1)S(1)} %copy-done.3, bf16[256,256]{1,0:T(8,128)(2,1)S(1)} %copy-done.2, bf16[256,256]{1,0:T(8,128)(2,1)S(1)} %copy-done.1, ...), custom_call_target="tpu_custom_call" | custom-call | tf_op jit(solution)/shard_map/correlate/pallas_call | solution.py:453
  67.5 29.0 %all_to_all.10.in_ref = bf16[32,2,64,128]{3,2,1,0:T(8,128)(2,1)S(1)} all-to-all(bf16[32,2,64,128]{3,2,1,0:T(8,128)(2,1)S(1)} %correlate.1), channel_id=1, replica_groups=mesh['z'=4,'x'=2,'y'=2,'core'=2] {'z','core','x','y'}, dimensions={0} | all-to-all | bytes 2097152 | tf_op jit(solution)/shard_map/all_to_all | solution.py:543
  96.5 0.0 copy-done.4
  96.5 0.0 copy-done.5
  96.5 2.1 %synthesise.1 = f32[2,32,32,256]{3,2,1,0:T(8,128)} custom-call(bf16[32,2,64,128]{3,2,1,0:T(8,128)(2,1)S(1)} %all_to_all.10.in_ref, bf16[256,256]{1,0:T(8,128)(2,1)S(1)} %copy-done.5, bf16[256,256]{1,0:T(8,128)(2,1)S(1)} %copy-done.4), custom_call_target="tpu_custom_call" | custom-call | tf_op jit(solution)/shard_map/synthesise/pallas_call | solution.py:518
Async XLA Ops:
  8.5 56.1 %copy-start = (bf16[256,256]{1,0:T(8,128)(2,1)S(1)}, bf16[256,256]{1,0:T(8,128)(2,1)}, u32[]{:S(2)}) copy-start(bf16[256,256]{1,0:T(8,128)(2,1)} %constant.41.clone.wzi_last_ref) | copy-start | bytes 393220
  8.5 56.1 %copy-start.1 = (bf16[256,256]{1,0:T(8,128)(2,1)S(1)}, bf16[256,256]{1,0:T(8,128)(2,1)}, u32[]{:S(2)}) copy-start(bf16[256,256]{1,0:T(8,128)(2,1)} %constant.40.clone.wz_last_ref) | copy-start | bytes 393220
  8.5 56.1 %copy-start.2 = (bf16[256,256]{1,0:T(8,128)(2,1)S(1)}, bf16[256,256]{1,0:T(8,128)(2,1)}, u32[]{:S(2)}) copy-start(bf16[256,256]{1,0:T(8,128)(2,1)} %constant.39.clone.wzi_ref) | copy-start | bytes 393220
  8.5 56.1 %copy-start.3 = (bf16[256,256]{1,0:T(8,128)(2,1)S(1)}, bf16[256,256]{1,0:T(8,128)(2,1)}, u32[]{:S(2)}) copy-start(bf16[256,256]{1,0:T(8,128)(2,1)} %constant.38.clone.wz_ref) | copy-start | bytes 393220
  8.6 56.1 %copy-start.6 = (s32[16,4]{0,1:T(4,128)S(1)}, s32[16,4]{0,1:T(4,128)}, u32[]{:S(2)}) copy-start(s32[16,4]{0,1:T(4,128)} %param.12) | copy-start | bytes 772
  8.6 56.0 %all-to-all-start = ((bf16[32,4,64,128]{3,2,1,0:T(8,128)(2,1)}), bf16[32,4,64,128]{3,2,1,0:T(8,128)(2,1)S(1)}, u32[]{:S(2)}, u32[]{:S(2)}) async-start(bf16[32,4,64,128]{3,2,1,0:T(8,128)(2,1)} %analyse.1), calls=%async_computation | async-start | bytes 4194304 | tf_op jit(solution)/shard_map/all_to_all | solution.py:541
  64.6 31.9 %copy-start.4 = (bf16[256,256]{1,0:T(8,128)(2,1)S(1)}, bf16[256,256]{1,0:T(8,128)(2,1)}, u32[]{:S(2)}) copy-start(bf16[256,256]{1,0:T(8,128)(2,1)} %constant.43.clone.wy_ref) | copy-start | bytes 393220
  64.6 31.9 %copy-start.5 = (bf16[256,256]{1,0:T(8,128)(2,1)S(1)}, bf16[256,256]{1,0:T(8,128)(2,1)}, u32[]{:S(2)}) copy-start(bf16[256,256]{1,0:T(8,128)(2,1)} %constant.42.clone.wx_ref) | copy-start | bytes 393220
